TPU v7x, 32 devices: a whole 2x2x4 slice. The times are simulated.
32 devices in a mesh: lat: 8 (over y, x, core), lon: 4 (over z).
Axes of the slice: x: 2, y: 2, z: 4, core: 2. Of those that a mesh axis runs over, the one named last changes fastest.
Arguments:
- state: float32 [256, 128, 512], P(None, 'lat', 'lon'), may hold values from -6 to 6
- north_coef: float32 [128, 512], P('lat', 'lon'), may hold values from 0.03 to 0.24
- east_coef: float32 [128, 512], P('lat', 'lon'), may hold values from 0.03 to 0.24
- land_mask: int32 [128, 512], P('lat', 'lon'), may hold values 0 or 1
- owner_slot: int32 [128, 512], P('lat', 'lon'), may hold values from 0 to 65535, as said below
- w_in: bfloat16 [512, 256], replicated, may hold values from -0.375 to 0.375
- w_mid: bfloat16 [512, 512], replicated, may hold values from -0.25 to 0.25
- w_out: bfloat16 [256, 512], replicated, may hold values from -0.25 to 0.25
- w_land: float32 [512], replicated, may hold values from -4 to 4
- tend_cot: bfloat16 [256, 65536], P(None, ('lat', 'lon')), may hold values from -6 to 6
Outputs:
- new_state: float32 [256, 128, 512], P(None, 'lat', 'lon')
- grad_in: float32 [512, 256], replicated
- grad_mid: float32 [512, 512], replicated
- grad_out: float32 [256, 512], replicated
- grad_land: float32 [512], replicated
Inputs may be any that keep to these rules, and one draw needn't show every extreme that they name: owner_slot holds each of its values once. Owner slot // 2048 counts devices along lat then lon, as tend_cot's columns are laid out. For a column in the 16 x 128 tile of device s (counted the same way), slot % 2048 // 64 equals s, so each device has exactly 64 columns for each owner.
All inputs are finite; a program needn't handle non-finite values. No bound on the sum of `land_mask` on one device may be relied on, other than what follows from the above.
Results may differ from a plain program's by a relative error of at most 0.0054.
Values may be sent and summed in bfloat16 or wider, within the bound.
A program may use at most 128 MiB of HBM per device.

v0:
```python
import jax
import jax.numpy as jnp
from jax import lax
from jax.sharding import PartitionSpec as P

SUBSTEPS = 3


def padded_2(array, sides, width, wrap):
    for axis, dim in sides:
        size, length = (lax.axis_size(axis), array.shape[dim])
        up = [(i, (i + 1) % size) for i in range(size if wrap else size - 1)]
        down = [(j, i) for i, j in up]
        last = lax.slice_in_dim(array, length - width, length, axis=dim)
        leading = lax.slice_in_dim(array, 0, width, axis=dim)
        before = lax.ppermute(last, axis, up)
        after = lax.ppermute(leading, axis, down)
        array = jnp.concatenate([before, array, after], axis=dim)
    return array


def advance(padded, north_face, east_face):
    flux_north = north_face[None, :-1, :] * (padded[:, 1:, :] - padded[:, :-1, :])
    flux_east = east_face[None, :, :-1] * (padded[:, :, 1:] - padded[:, :, :-1])
    inner = padded[:, 1:-1, 1:-1]
    return (
        inner
        + flux_north[:, 1:, 1:-1]
        - flux_north[:, :-1, 1:-1]
        + flux_east[:, 1:-1, 1:]
        - flux_east[:, 1:-1, :-1]
    )


def physics(feeds, land, cot_cols, w_in, w_mid, w_out, w_land):
    pre_first = (
        jnp.dot(w_in, feeds, preferred_element_type=jnp.float32)
        + w_land[:, None] * land.astype(jnp.float32)[None, :]
    )
    sig_first = jax.nn.sigmoid(pre_first)
    act_first = (pre_first * sig_first).astype(jnp.bfloat16)
    pre_second = jnp.dot(w_mid, act_first, preferred_element_type=jnp.float32)
    sig_second = jax.nn.sigmoid(pre_second)
    act_second = (pre_second * sig_second).astype(jnp.bfloat16)
    tendency = jnp.dot(w_out, act_second, preferred_element_type=jnp.float32).astype(jnp.bfloat16)
    grad_out = jnp.dot(cot_cols, act_second.T, preferred_element_type=jnp.float32)
    back_second = (
        jnp.dot(w_out.T, cot_cols, preferred_element_type=jnp.float32)
        * sig_second
        * (1.0 + pre_second * (1.0 - sig_second))
    ).astype(jnp.bfloat16)
    grad_mid = jnp.dot(back_second, act_first.T, preferred_element_type=jnp.float32)
    back_first = (
        jnp.dot(w_mid.T, back_second, preferred_element_type=jnp.float32)
        * sig_first
        * (1.0 + pre_first * (1.0 - sig_first))
    ).astype(jnp.bfloat16)
    grad_in = jnp.dot(back_first, feeds.T, preferred_element_type=jnp.float32)
    grad_land = jnp.dot(back_first, land, preferred_element_type=jnp.float32)
    return (tendency, (grad_in, grad_mid, grad_out, grad_land))


def per_device(
    state, north_coef, east_coef, land_mask, owner_slot, w_in, w_mid, w_out, w_land, tend_cot
):
    channels, tile_rows, tile_cols = state.shape
    lat_count = lax.axis_size("lat")
    dev_count = lat_count * lax.axis_size("lon")
    columns = tile_rows * tile_cols
    per_owner = columns // dev_count
    row_index = lax.axis_index("lat") * tile_rows + jnp.arange(tile_rows, dtype=jnp.int32)
    north_face = jnp.where(
        row_index[:, None] < tile_rows * lat_count - 1, north_coef, jnp.float32(0.0)
    )
    coefs = jnp.stack([north_face, east_coef])
    field = state
    for step in range(SUBSTEPS):
        joined = jnp.concatenate([field, coefs], 0)
        joined = padded_2(joined, (("lat", 1),), 1, False)
        joined = padded_2(joined, (("lon", 2),), 1, True)
        field = advance(joined[:channels], joined[channels], joined[channels + 1])
    dynamic = field.reshape(channels, columns)
    slots = owner_slot.reshape(columns)
    place = slots // columns * per_owner + slots % per_owner
    order = jnp.zeros((columns,), jnp.int32).at[place].set(jnp.arange(columns, dtype=jnp.int32))
    land_row = land_mask.reshape(1, columns).astype(jnp.bfloat16)
    send_feeds = jnp.take(dynamic.astype(jnp.bfloat16), order, axis=1)
    send_land = jnp.take(land_row, order, axis=1)
    owned_feeds, owned_land = (
        lax.all_to_all(send_feeds, ("lat", "lon"), split_axis=1, concat_axis=1, tiled=True),
        lax.all_to_all(send_land, ("lat", "lon"), split_axis=1, concat_axis=1, tiled=True),
    )
    owned_tend, gradients = physics(
        owned_feeds, owned_land[0], tend_cot, w_in, w_mid, w_out, w_land
    )
    tend_back = lax.all_to_all(owned_tend, ("lat", "lon"), split_axis=1, concat_axis=1, tiled=True)
    tendency = jnp.take(tend_back, place, axis=1)
    new_state = (dynamic + tendency.astype(jnp.float32)).reshape(channels, tile_rows, tile_cols)
    summed = lax.psum((gradients[0], gradients[1], gradients[2], gradients[3]), ("lat", "lon"))
    scale = jnp.float32((columns * dev_count) ** (-0.5))
    return (new_state, summed[0] * scale, summed[1] * scale, summed[2] * scale, summed[3] * scale)


def solution(mesh):
    placed = (
        P(None, "lat", "lon"),
        P("lat", "lon"),
        P("lat", "lon"),
        P("lat", "lon"),
        P("lat", "lon"),
        P(),
        P(),
        P(),
        P(),
        P(None, ("lat", "lon")),
    )
    return jax.shard_map(
        per_device,
        mesh=mesh,
        in_specs=placed,
        out_specs=(P(None, "lat", "lon"), P(), P(), P(), P()),
        check_vma=False,
    )
```

profile of v0, /device:TPU:0, one launch (start us, length us, event | category | flops | bytes accessed | tf_op | source)
XLA Modules:
  0.0 481.1 jit_solution(4121167742384346477)
XLA Ops:
  14.0 3.9 collective-permute-done.1
  22.1 3.7 copy.51
  37.2 4.2 copy.54
  41.4 9.9 %fusion.3 = f32[258,18,130]{2,1,0:T(8,128)S(1)} fusion(f32[1,16,128]{2,1,0:T(8,128)S(1)} %bitcast.125, f32[1,16,128]{2,1,0:T(8,128)S(1)} %select_bitcast_fusion, f32[258,18,1]{2,1,0:T(8,128)} %copy.54, f32[258,1,128]{2,1,0:T(1,128)S(1)} %copy.50, f32[256,16,128]{2,1,0:T(8,128)S(1)} %copy-done.2, f32[258,1,128]{2,1,0:T(1,128)S(1)} %copy.49, ...), kind=kLoop, calls=%fused_computation.25 | loop fusion | flops 3622320 | bytes 4829760 | tf_op jit(solution)/shard_map/concatenate | solution.py:18
  55.0 14.3 %fusion.16 = f32[256,18,129]{2,1,0:T(8,128)} fusion(f32[1,16,128]{2,1,0:T(8,128)S(1)} %bitcast.126, f32[1,16,128]{2,1,0:T(8,128)S(1)} %select_bitcast_fusion, f32[258,18,1]{2,1,0:T(8,128)S(1)} %copy-done.5, f32[258,1,128]{2,1,0:T(1,128)S(1)} %copy.50, f32[258,1,128]{2,1,0:T(1,128)S(1)} %copy.49, f32[256,16,128]{2,1,0:T(8,128)S(1)} %copy-done.2, ...), kind=kLoop, calls=%fused_computation.38 | loop fusion | flops 7133184 | bytes 4801896 | tf_op jit(solution)/shard_map/mul | solution.py:24
  69.2 8.6 %slice_subtract_fusion.7 = f32[256,16,128]{2,1,0:T(8,128)S(1)} fusion(f32[256,18,129]{2,1,0:T(8,128)} %fusion.16, f32[256,17,130]{2,1,0:T(8,128)} %fusion.38, f32[256,16,128]{2,1,0:T(8,128)S(1)} %copy-done.3), kind=kLoop, calls=%fused_computation.107 | loop fusion | flops 2097152 | bytes 12582912 | tf_op jit(solution)/shard_map/sub | solution.py:27
  79.1 5.4 %collective-permute-start.4 = (f32[258,1,128]{2,0,1:T(8,128)}, f32[258,1,128]{2,0,1:T(8,128)S(1)}, u32[]{:S(2)}, u32[]{:S(2)}) collective-permute-start(f32[258,1,128]{2,0,1:T(8,128)} %copy.57), channel_id=1, source_target_pairs={{0,4},{4,8},{8,12},{12,16},{16,20},{20,24},{24,28},{1,5},{5,9},{9,... | collective-permute-start | bytes 396296 | tf_op jit(solution)/shard_map/ppermute | solution.py:16
  86.6 8.0 %scatter_custom_fusion = s32[2048]{0:T(1024)S(1)} fusion(s32[2048]{0:T(1024)S(1)} %bitcast.140, s32[2048]{0:T(1024)S(1)} %iota.9, s32[]{:T(128)} %constant.67.clone.1), kind=kCustom, calls=%fused_computation.154 | custom fusion | bytes 8196 | tf_op jit(solution)/shard_map/scatter | solution.py:85
  99.9 3.7 copy.61
  103.7 4.4 copy.62
  108.0 3.8 collective-permute-start.7
  115.4 4.2 copy.64
  119.7 9.9 %fusion.7 = f32[258,18,130]{2,1,0:T(8,128)S(1)} fusion(f32[1,16,128]{2,1,0:T(8,128)S(1)} %bitcast.129, f32[1,16,128]{2,1,0:T(8,128)S(1)} %select_bitcast_fusion, f32[258,18,1]{2,1,0:T(8,128)} %copy.64, f32[258,1,128]{2,1,0:T(1,128)S(1)} %copy.60, f32[256,16,128]{2,1,0:T(8,128)S(1)} %slice_subtract_fusion.7, f32[258,1,128]{2,1,0:T(1,128)S(1)} %copy.59, ...), kind=kLoop, calls=%fused_computation.29 | loop fusion | flops 3622320 | bytes 4829760 | tf_op jit(solution)/shard_map/concatenate | solution.py:18
  129.6 4.1 fusion.37
  134.5 12.7 %fusion.21 = f32[256,18,129]{2,1,0:T(8,128)} fusion(f32[1,16,128]{2,1,0:T(8,128)S(1)} %bitcast.130, f32[1,16,128]{2,1,0:T(8,128)S(1)} %select_bitcast_fusion, f32[258,18,1]{2,1,0:T(8,128)S(1)} %copy-done.6, f32[258,1,128]{2,1,0:T(1,128)S(1)} %copy.60, f32[258,1,128]{2,1,0:T(1,128)S(1)} %copy.59, f32[256,16,128]{2,1,0:T(8,128)S(1)} %slice_subtract_fusion.7, ...), kind=kLoop, calls=%fused_computation.43 | loop fusion | flops 7133184 | bytes 4801896 | tf_op jit(solution)/shard_map/mul | solution.py:24
  147.2 9.0 %slice_subtract_fusion.5 = f32[256,16,128]{2,1,0:T(8,128)S(1)} fusion(f32[256,18,129]{2,1,0:T(8,128)} %fusion.21, f32[256,17,130]{2,1,0:T(8,128)} %fusion.37, f32[256,16,128]{2,1,0:T(8,128)} %copy-done.1), kind=kLoop, calls=%fused_computation.103 | loop fusion | flops 2097152 | bytes 12582912 | tf_op jit(solution)/shard_map/sub | solution.py:27
  161.9 13.1 %gather_fusion = bf16[2048]{0:T(1024)(128)(2,1)S(1)} fusion(bf16[2048]{0:T(1024)(128)(2,1)S(1)} %convert_bitcast_fusion, s32[2048]{0:T(1024)S(1)} %fusion.61), kind=kCustom, calls=%fused_computation.2 | custom fusion | bytes 16384 | tf_op jit(solution)/shard_map/jit(_take)/gather | solution.py:88
  184.0 4.4 copy.72
  188.4 3.8 collective-permute-start.11
  192.9 7.6 %all-to-all-start.1 = ((bf16[1,32,64]{2,0,1:T(2,128)(2,1)}), bf16[1,32,64]{2,0,1:T(2,128)(2,1)S(1)}, u32[]{:S(2)}, u32[]{:S(2)}) async-start(bf16[1,32,64]{2,0,1:T(2,128)(2,1)} %reshape.263), calls=%async_computation.1 | async-start | bytes 32768 | tf_op jit(solution)/shard_map/all_to_all | solution.py:91
  204.1 4.2 copy.74
  208.3 9.9 %fusion.11 = f32[258,18,130]{2,1,0:T(8,128)S(1)} fusion(f32[1,16,128]{2,1,0:T(8,128)S(1)} %bitcast.133, f32[1,16,128]{2,1,0:T(8,128)S(1)} %select_bitcast_fusion, f32[258,18,1]{2,1,0:T(8,128)} %copy.74, f32[258,1,128]{2,1,0:T(1,128)S(1)} %copy.70, f32[256,16,128]{2,1,0:T(8,128)S(1)} %slice_subtract_fusion.5, f32[258,1,128]{2,1,0:T(1,128)S(1)} %copy.69, ...), kind=kLoop, calls=%fused_computation.33 | loop fusion | flops 3622320 | bytes 4829760 | tf_op jit(solution)/shard_map/concatenate | solution.py:18
  218.3 4.1 fusion.36
  223.2 12.7 %fusion.26 = f32[256,18,129]{2,1,0:T(8,128)} fusion(f32[1,16,128]{2,1,0:T(8,128)S(1)} %bitcast.134, f32[1,16,128]{2,1,0:T(8,128)S(1)} %select_bitcast_fusion, f32[258,18,1]{2,1,0:T(8,128)S(1)} %copy-done.4, f32[258,1,128]{2,1,0:T(1,128)S(1)} %copy.70, f32[258,1,128]{2,1,0:T(1,128)S(1)} %copy.69, f32[256,16,128]{2,1,0:T(8,128)S(1)} %slice_subtract_fusion.5, ...), kind=kLoop, calls=%fused_computation.48 | loop fusion | flops 7133184 | bytes 4801896 | tf_op jit(solution)/shard_map/mul | solution.py:24
  235.9 9.8 %slice_subtract_fusion.3 = f32[256,16,128]{2,1,0:T(8,128)} fusion(f32[256,18,129]{2,1,0:T(8,128)} %fusion.26, f32[256,17,130]{2,1,0:T(8,128)} %fusion.36, f32[256,16,128]{2,1,0:T(8,128)S(1)} %slice_subtract_fusion.5), kind=kLoop, calls=%fused_computation.99 | loop fusion | flops 2097152 | bytes 12582912 | tf_op jit(solution)/shard_map/sub | solution.py:27
  250.4 7.5 %gather_fusion.1 = bf16[2048,256]{1,0:T(8,128)(2,1)S(1)} fusion(bf16[256,2048]{0,1:T(8,128)(2,1)S(1)} %bitcast_convert_fusion, s32[2048]{0:T(1024)S(1)} %fusion.61), kind=kCustom, calls=%fused_computation.clone | custom fusion | bytes 2105344 | tf_op jit(solution)/shard_map/jit(_take)/gather | solution.py:87
  259.2 5.8 %all-to-all-start = ((bf16[256,32,64]{0,2,1:T(8,128)(2,1)}), bf16[256,32,64]{0,2,1:T(8,128)(2,1)S(1)}, u32[]{:S(2)}, u32[]{:S(2)}) async-start(bf16[256,32,64]{0,2,1:T(8,128)(2,1)} %bitcast.13), calls=%async_computation | async-start | bytes 2097152 | tf_op jit(solution)/shard_map/all_to_all | solution.py:90
  265.2 24.9 %all-to-all-done = bf16[256,32,64]{0,2,1:T(8,128)(2,1)S(1)} async-done(((bf16[256,32,64]{0,2,1:T(8,128)(2,1)}), bf16[256,32,64]{0,2,1:T(8,128)(2,1)S(1)}, u32[]{:S(2)}, u32[]{:S(2)}) %all-to-all-start) | async-done | bytes 1048608 | tf_op jit(solution)/shard_map/all_to_all | solution.py:90
  304.1 4.5 all-to-all-start.2
  313.9 47.0 %psum.31 = f32[512]{0:T(512)S(1)} all-reduce(f32[512]{0:T(512)S(1)} %bitcast.139), channel_id=1, replica_groups=mesh['lat'=8,'lon'=4] {'lat','lon'}, use_global_device_ids=true, to_apply=%region_4.6 | all-reduce | flops 512 | bytes 4096 | tf_op jit(solution)/shard_map/psum | solution.py:99
  361.5 93.3 %all-reduce.3.cloned.1.call-done = (f32[512,256]{1,0:T(8,128)}, f32[512,512]{1,0:T(8,128)}, f32[256,512]{0,1:T(8,128)}) async-done(((f32[512,256]{1,0:T(8,128)}, f32[512,512]{1,0:T(8,128)}, f32[256,512]{0,1:T(8,128)}), (f32[512,256]{1,0:T(8,128)}, f32[512,512]{1,0:T(8,128)}, f32[256,512]{0,1:T(8,128)})) %all-reduce.3.cloned.1.call-update) | async-done | bytes 2097168 | tf_op jit(solution)/shard_map/psum | solution.py:99
  461.0 9.1 %gather_fusion.2 = bf16[2048,256]{1,0:T(8,128)(2,1)} fusion(bf16[256,2048]{0,1:T(8,128)(2,1)S(1)} %bitcast.118, s32[2048]{0:T(1024)S(1)} %broadcast_clamp_fusion), kind=kCustom, calls=%fused_computation.1.clone | custom fusion | bytes 2105344 | tf_op jit(solution)/shard_map/jit(_take)/gather | solution.py:97
  (125 shorter events, 94.9 us)
Async XLA Ops:
  7.2 286.2 %copy-start = (bf16[256,2048]{1,0:T(8,128)(2,1)S(1)}, bf16[256,2048]{1,0:T(8,128)(2,1)}, u32[]{:S(2)}) copy-start(bf16[256,2048]{1,0:T(8,128)(2,1)} %param.21) | copy-start | bytes 3145732
  7.2 10.8 %copy-start.9 = (f32[16,128]{1,0:T(8,128)S(1)}, f32[16,128]{1,0:T(8,128)}, u32[]{:S(2)}) copy-start(f32[16,128]{1,0:T(8,128)} %param.14) | copy-start | bytes 24580
  7.2 10.8 %copy-start.2 = (f32[256,16,128]{2,1,0:T(8,128)S(1)}, f32[256,16,128]{2,1,0:T(8,128)}, u32[]{:S(2)}) copy-start(f32[256,16,128]{2,1,0:T(8,128)} %param.12) | copy-start | bytes 6291460
  10.1 3.7 collective-permute-start
  12.5 5.3 %collective-permute-start.1 = (f32[258,1,128]{2,0,1:T(8,128)S(1)}, f32[258,1,128]{2,0,1:T(8,128)S(1)}, u32[]{:S(2)}, u32[]{:S(2)}) collective-permute-start(f32[258,1,128]{2,0,1:T(8,128)S(1)} %copy.48), channel_id=1, source_target_pairs={{4,0},{8,4},{12,8},{16,12},{20,16},{24,20},{28,24},{5,1},{9,5},{13... | collective-permute-start | bytes 396296 | tf_op jit(solution)/shard_map/ppermute | solution.py:17
  25.8 7.8 %collective-permute-start.2 = (f32[258,18,1]{0,1,2:T(8,128)S(1)}, f32[258,18,1]{0,1,2:T(8,128)S(1)}, u32[]{:S(2)}, u32[]{:S(2)}) collective-permute-start(f32[258,18,1]{0,1,2:T(8,128)S(1)} %copy.51), channel_id=1, source_target_pairs={{0,1},{1,2},{2,3},{3,0},{4,5},{5,6},{6,7},{7,4},{8,9},{9,10},{10,1... | collective-permute-start | bytes 55736 | tf_op jit(solution)/shard_map/ppermute | solution.py:16
  31.2 6.0 %collective-permute-start.3 = (f32[258,18,1]{0,1,2:T(8,128)S(1)}, f32[258,18,1]{0,1,2:T(8,128)}, u32[]{:S(2)}, u32[]{:S(2)}) collective-permute-start(f32[258,18,1]{0,1,2:T(8,128)S(1)} %copy.52), channel_id=1, source_target_pairs={{1,0},{2,1},{3,2},{0,3},{5,4},{6,5},{7,6},{4,7},{9,8},{10,9},{11,1... | collective-permute-start | bytes 55736 | tf_op jit(solution)/shard_map/ppermute | solution.py:17
  51.3 3.6 copy-start.5
  55.0 14.3 %copy-start.3 = (f32[256,16,128]{2,1,0:T(8,128)S(1)}, f32[256,16,128]{2,1,0:T(8,128)}, u32[]{:S(2)}) copy-start(f32[256,16,128]{2,1,0:T(8,128)} %param.12) | copy-start | bytes 6291460
  77.8 56.0 %copy-start.1 = (f32[256,16,128]{2,1,0:T(8,128)}, f32[256,16,128]{2,1,0:T(8,128)S(1)}, u32[]{:S(2)}) copy-start(f32[256,16,128]{2,1,0:T(8,128)S(1)} %slice_subtract_fusion.7) | copy-start | bytes 6291460
  77.8 8.7 %copy-start.11 = (s32[16,128]{1,0:T(8,128)S(1)}, s32[16,128]{1,0:T(8,128)}, u32[]{:S(2)}) copy-start(s32[16,128]{1,0:T(8,128)} %param.16) | copy-start | bytes 24580
  79.1 15.5 %collective-permute-start.4 = (f32[258,1,128]{2,0,1:T(8,128)}, f32[258,1,128]{2,0,1:T(8,128)S(1)}, u32[]{:S(2)}, u32[]{:S(2)}) collective-permute-start(f32[258,1,128]{2,0,1:T(8,128)} %copy.57), channel_id=1, source_target_pairs={{0,4},{4,8},{8,12},{12,16},{16,20},{20,24},{24,28},{1,5},{5,9},{9,... | collective-permute-start | bytes 396296 | tf_op jit(solution)/shard_map/ppermute | solution.py:16
  85.2 9.6 %collective-permute-start.5 = (f32[258,1,128]{2,0,1:T(8,128)}, f32[258,1,128]{2,0,1:T(8,128)}, u32[]{:S(2)}, u32[]{:S(2)}) collective-permute-start(f32[258,1,128]{2,0,1:T(8,128)} %copy.58), channel_id=1, source_target_pairs={{4,0},{8,4},{12,8},{16,12},{20,16},{24,20},{28,24},{5,1},{9,5},{13... | collective-permute-start | bytes 396296 | tf_op jit(solution)/shard_map/ppermute | solution.py:17
  103.6 8.2 %collective-permute-start.6 = (f32[258,18,1]{0,1,2:T(8,128)S(1)}, f32[258,18,1]{0,1,2:T(8,128)S(1)}, u32[]{:S(2)}, u32[]{:S(2)}) collective-permute-start(f32[258,18,1]{0,1,2:T(8,128)S(1)} %copy.61), channel_id=1, source_target_pairs={{0,1},{1,2},{2,3},{3,0},{4,5},{5,6},{6,7},{7,4},{8,9},{9,10},{10,1... | collective-permute-start | bytes 55736 | tf_op jit(solution)/shard_map/ppermute | solution.py:16
  108.0 7.4 %collective-permute-start.7 = (f32[258,18,1]{0,1,2:T(8,128)}, f32[258,18,1]{0,1,2:T(8,128)}, u32[]{:S(2)}, u32[]{:S(2)}) collective-permute-start(f32[258,18,1]{0,1,2:T(8,128)} %copy.62), channel_id=1, source_target_pairs={{1,0},{2,1},{3,2},{0,3},{5,4},{6,5},{7,6},{4,7},{9,8},{10,9},{11,1... | collective-permute-start | bytes 55736 | tf_op jit(solution)/shard_map/ppermute | solution.py:17
  129.6 4.1 copy-start.6
  129.6 4.9 %copy-start.8 = (f32[258,18,1]{2,1,0:T(8,128)S(1)}, f32[258,18,1]{2,1,0:T(8,128)}, u32[]{:S(2)}) copy-start(f32[258,18,1]{2,1,0:T(8,128)} %copy.64) | copy-start | bytes 55732
  156.2 5.6 %copy-start.12 = (s32[16,128]{1,0:T(8,128)S(1)}, s32[16,128]{1,0:T(8,128)}, u32[]{:S(2)}) copy-start(s32[16,128]{1,0:T(8,128)} %param.15) | copy-start | bytes 24580
  157.3 17.7 %collective-permute-start.8 = (f32[258,1,128]{2,0,1:T(8,128)}, f32[258,1,128]{2,0,1:T(8,128)S(1)}, u32[]{:S(2)}, u32[]{:S(2)}) collective-permute-start(f32[258,1,128]{2,0,1:T(8,128)} %copy.67), channel_id=1, source_target_pairs={{0,4},{4,8},{8,12},{12,16},{16,20},{20,24},{24,28},{1,5},{5,9},{9,... | collective-permute-start | bytes 396296 | tf_op jit(solution)/shard_map/ppermute | solution.py:16
  160.4 14.7 %collective-permute-start.9 = (f32[258,1,128]{2,0,1:T(8,128)}, f32[258,1,128]{2,0,1:T(8,128)}, u32[]{:S(2)}, u32[]{:S(2)}) collective-permute-start(f32[258,1,128]{2,0,1:T(8,128)} %copy.68), channel_id=1, source_target_pairs={{4,0},{8,4},{12,8},{16,12},{20,16},{24,20},{28,24},{5,1},{9,5},{13... | collective-permute-start | bytes 396296 | tf_op jit(solution)/shard_map/ppermute | solution.py:17
  184.0 16.5 %collective-permute-start.10 = (f32[258,18,1]{0,1,2:T(8,128)S(1)}, f32[258,18,1]{0,1,2:T(8,128)S(1)}, u32[]{:S(2)}, u32[]{:S(2)}) collective-permute-start(f32[258,18,1]{0,1,2:T(8,128)S(1)} %copy.71), channel_id=1, source_target_pairs={{0,1},{1,2},{2,3},{3,0},{4,5},{5,6},{6,7},{7,4},{8,9},{9,10},{10,1... | collective-permute-start | bytes 55736 | tf_op jit(solution)/shard_map/ppermute | solution.py:16
  188.4 15.7 %collective-permute-start.11 = (f32[258,18,1]{0,1,2:T(8,128)}, f32[258,18,1]{0,1,2:T(8,128)}, u32[]{:S(2)}, u32[]{:S(2)}) collective-permute-start(f32[258,18,1]{0,1,2:T(8,128)} %copy.72), channel_id=1, source_target_pairs={{1,0},{2,1},{3,2},{0,3},{5,4},{6,5},{7,6},{4,7},{9,8},{10,9},{11,1... | collective-permute-start | bytes 55736 | tf_op jit(solution)/shard_map/ppermute | solution.py:17
  192.9 66.3 %all-to-all-start.1 = ((bf16[1,32,64]{2,0,1:T(2,128)(2,1)}), bf16[1,32,64]{2,0,1:T(2,128)(2,1)S(1)}, u32[]{:S(2)}, u32[]{:S(2)}) async-start(bf16[1,32,64]{2,0,1:T(2,128)(2,1)} %reshape.263), calls=%async_computation.1 | async-start | bytes 32768 | tf_op jit(solution)/shard_map/all_to_all | solution.py:91
  218.2 4.1 copy-start.4
  218.3 4.9 %copy-start.7 = (f32[258,18,1]{2,1,0:T(8,128)S(1)}, f32[258,18,1]{2,1,0:T(8,128)}, u32[]{:S(2)}) copy-start(f32[258,18,1]{2,1,0:T(8,128)} %copy.74) | copy-start | bytes 55732
  258.0 32.2 %copy-start.14 = (bf16[512,256]{1,0:T(8,128)(2,1)S(1)}, bf16[512,256]{1,0:T(8,128)(2,1)}, u32[]{:S(2)}) copy-start(bf16[512,256]{1,0:T(8,128)(2,1)} %param.17) | copy-start | bytes 786436
  258.0 32.2 %copy-start.15 = (f32[512]{0:T(512)S(1)}, f32[512]{0:T(512)}, u32[]{:S(2)}) copy-start(f32[512]{0:T(512)} %param.20) | copy-start | bytes 6148
  259.2 30.9 %all-to-all-start = ((bf16[256,32,64]{0,2,1:T(8,128)(2,1)}), bf16[256,32,64]{0,2,1:T(8,128)(2,1)S(1)}, u32[]{:S(2)}, u32[]{:S(2)}) async-start(bf16[256,32,64]{0,2,1:T(8,128)(2,1)} %bitcast.13), calls=%async_computation | async-start | bytes 2097152 | tf_op jit(solution)/shard_map/all_to_all | solution.py:90
  290.1 1.4 copy-start.13
  291.5 3.5 copy-start.10
  304.1 156.8 %all-to-all-start.2 = ((bf16[256,32,64]{0,2,1:T(8,128)(2,1)}), bf16[256,32,64]{0,2,1:T(8,128)(2,1)S(1)}, u32[]{:S(2)}, u32[]{:S(2)}) async-start(bf16[256,32,64]{0,2,1:T(8,128)(2,1)} %bitcast.122), calls=%async_computation.2 | async-start | bytes 2097152 | tf_op jit(solution)/shard_map/all_to_all | solution.py:96
  308.6 146.1 %all-reduce.3.cloned.1.call-start = ((), (), s32[]{:S(2)}) async-start(), calls=%async_computation.3 | async-start | bytes 4194304 | tf_op jit(solution)/shard_map/psum | solution.py:99
Sparse Core Ops, SparseCore 0:
  315.6 139.0 all-reduce.2
where the time goes:
time: 486 us; the launch traced here: 481 us
  other arithmetic  124 us (26%)
  waiting for transfers between devices  122 us (25%)
  local copies, waits for them, and re-layouts  110 us (23%)
  blocking collectives  47 us (10%)
  starting transfers between devices  44 us (9%)
  matrix products  19 us (4%)
  between operations  14.9 us (3%)
    psum x1, waiting for transfers between devices, per_device(): lax.psum((gradients[0], gradients[1], gradients[2], gradients[3]), ('lat'...  93.3 us
    psum x1, blocking collectives, per_device(): lax.psum((gradients[0], gradients[1], gradients[2], gradients[3]), ('lat'...  47 us
    mul x3, other arithmetic, advance(): flux_east = east_face[None, :, :-1] * (padded[:, :, 1:] - padded[:, :, :-1])  39.6 us
    concatenate x6, other arithmetic, padded_2(): array = jnp.concatenate([before, array, after], axis=dim)  31.2 us
    sub x3, other arithmetic, advance(): inner + flux_north[:, 1:, 1:-1] - flux_north[:, :-1, 1:-1]  27.3 us
    all_to_all x1, waiting for transfers between devices, per_device(): lax.all_to_all(send_feeds, ('lat', 'lon'), split_axis=1, concat_axis=1, t...  24.9 us
    slice x9, local copies, waits for them, and re-layouts, padded_2(): leading = lax.slice_in_dim(array, 0, width, axis=dim)  24.5 us
    ppermute x6, local copies, waits for them, and re-layouts, padded_2(): after = lax.ppermute(leading, axis, down)  14.9 us
  transfers between devices with their start and end apart: 16, of which 3 were waited for; matrix products, arithmetic and copies ran while one was open for 24% of the time, Pallas kernels for 0%

commit v1 on v0

--- a/solution.py
+++ b/solution.py
@@ -68,37 +68,37 @@
     dev_count = lat_count * lax.axis_size("lon")
     columns = tile_rows * tile_cols
     per_owner = columns // dev_count
+    cot_rows = tend_cot.T.reshape(dev_count, per_owner, channels)
+    cot_rows = lax.all_to_all(cot_rows, ("lat", "lon"), split_axis=0, concat_axis=0, tiled=True)
+    cot_rows = cot_rows.reshape(columns, channels)
     row_index = lax.axis_index("lat") * tile_rows + jnp.arange(tile_rows, dtype=jnp.int32)
     north_face = jnp.where(
         row_index[:, None] < tile_rows * lat_count - 1, north_coef, jnp.float32(0.0)
     )
     coefs = jnp.stack([north_face, east_coef])
-    field = state
+    joined = jnp.concatenate([state, coefs], 0)
+    joined = padded_2(joined, (("lat", 1),), SUBSTEPS, False)
+    joined = padded_2(joined, (("lon", 2),), SUBSTEPS, True)
+    field = joined[:channels]
+    north, east = joined[channels], joined[channels + 1]
     for step in range(SUBSTEPS):
-        joined = jnp.concatenate([field, coefs], 0)
-        joined = padded_2(joined, (("lat", 1),), 1, False)
-        joined = padded_2(joined, (("lon", 2),), 1, True)
-        field = advance(joined[:channels], joined[channels], joined[channels + 1])
+        field = advance(field, north, east)
+        north, east = north[1:-1, 1:-1], east[1:-1, 1:-1]
     dynamic = field.reshape(channels, columns)
     slots = owner_slot.reshape(columns)
     place = slots // columns * per_owner + slots % per_owner
-    order = jnp.zeros((columns,), jnp.int32).at[place].set(jnp.arange(columns, dtype=jnp.int32))
-    land_row = land_mask.reshape(1, columns).astype(jnp.bfloat16)
-    send_feeds = jnp.take(dynamic.astype(jnp.bfloat16), order, axis=1)
-    send_land = jnp.take(land_row, order, axis=1)
-    owned_feeds, owned_land = (
-        lax.all_to_all(send_feeds, ("lat", "lon"), split_axis=1, concat_axis=1, tiled=True),
-        lax.all_to_all(send_land, ("lat", "lon"), split_axis=1, concat_axis=1, tiled=True),
+    pick = (jnp.arange(columns, dtype=jnp.int32)[:, None] == place[None, :]).astype(jnp.bfloat16)
+    land = land_mask.reshape(columns).astype(jnp.bfloat16)
+    cot_grid = lax.dot_general(
+        cot_rows, pick, (((0,), (0,)), ((), ())), preferred_element_type=jnp.float32
+    ).astype(jnp.bfloat16)
+    tendency, gradients = physics(
+        dynamic.astype(jnp.bfloat16), land, cot_grid, w_in, w_mid, w_out, w_land
     )
-    owned_tend, gradients = physics(
-        owned_feeds, owned_land[0], tend_cot, w_in, w_mid, w_out, w_land
-    )
-    tend_back = lax.all_to_all(owned_tend, ("lat", "lon"), split_axis=1, concat_axis=1, tiled=True)
-    tendency = jnp.take(tend_back, place, axis=1)
     new_state = (dynamic + tendency.astype(jnp.float32)).reshape(channels, tile_rows, tile_cols)
-    summed = lax.psum((gradients[0], gradients[1], gradients[2], gradients[3]), ("lat", "lon"))
     scale = jnp.float32((columns * dev_count) ** (-0.5))
-    return (new_state, summed[0] * scale, summed[1] * scale, summed[2] * scale, summed[3] * scale)
+    summed = lax.psum(gradients, ("lat", "lon"))
+    return (new_state,) + tuple(g * scale for g in summed)
 
 
 def solution(mesh):

time: 486 us -> 323 us (0.66)
  local copies, waits for them, and re-layouts: 110 us -> 32.9 us
  other arithmetic: 124 us -> 89.3 us
  waiting for transfers between devices: 122 us -> 91.9 us
  starting transfers between devices: 44 us -> 17.3 us
  matrix products: 19 us -> 27 us
    gather x3 -> x0, local copies, waits for them, and re-layouts: 29.6 us -> none  [the longest x1 13.1 us: per_device(): send_land = jnp.take(land_row, order, axis=1)]
    mul x3, other arithmetic: 39.6 us -> 13 us  [advance(): flux_east = east_face[None, :, :-1] * (padded[:, :, 1:] - padded[:, :, :-1])]
    all_to_all x3 -> x1, waiting for transfers between devices: 24.9 us -> 0.01 us  [per_device(): lax.all_to_all(cot_rows, ('lat', 'lon'), split_axis=0, concat_axis=0, til...]
    slice x9 -> x2, local copies, waits for them, and re-layouts: 24.5 us -> 4.53 us  [padded_2(): leading = lax.slice_in_dim(array, 0, width, axis=dim)]
    concatenate x6 -> x2, other arithmetic: 31.2 us -> 11.9 us  [padded_2(): array = jnp.concatenate([before, array, after], axis=dim)]
    sub x3, other arithmetic: 27.3 us -> 43.2 us  [advance(): inner + flux_north[:, 1:, 1:-1] - flux_north[:, :-1, 1:-1]]
    ppermute x6 -> x2, starting transfers between devices: 14.1 us -> 3.63 us  [padded_2(): after = lax.ppermute(leading, axis, down)]
    ppermute x6 -> x2, local copies, waits for them, and re-layouts: 14.9 us -> 5.48 us  [padded_2(): after = lax.ppermute(leading, axis, down)]
  transfers between devices with their start and end apart: 16 -> 6, of which waited for: 3 -> 2; matrix products, arithmetic and copies ran while one was open for 24% -> 38% of each run, Pallas kernels for 0% -> 0%
where the time goes in v1:
time: 323 us; the launch traced here: 318 us
  waiting for transfers between devices  91.9 us (28%)
  other arithmetic  89.3 us (28%)
  blocking collectives  45 us (14%)
  local copies, waits for them, and re-layouts  32.9 us (10%)
  matrix products  27 us (8%)
  starting transfers between devices  17.3 us (5%)
  between operations  14.6 us (5%)
    psum x1, waiting for transfers between devices, per_device(): summed = lax.psum(gradients, ('lat', 'lon'))  86.8 us
    psum x1, blocking collectives, per_device(): summed = lax.psum(gradients, ('lat', 'lon'))  45 us
    sub x3, other arithmetic, advance(): inner + flux_north[:, 1:, 1:-1] - flux_north[:, :-1, 1:-1]  43.2 us
    mul x3, other arithmetic, advance(): flux_east = east_face[None, :, :-1] * (padded[:, :, 1:] - padded[:, :, :-1])  13 us
    concatenate x2, other arithmetic, padded_2(): array = jnp.concatenate([before, array, after], axis=dim)  11.9 us
    mul x4, other arithmetic, advance(): north_face[None, :-1, :] * (padded[:, 1:, :] - padded[:, :-1, :])  11.3 us
    unnamed x54, local copies, waits for them, and re-layouts  9.52 us
    all_to_all x1, starting transfers between devices, per_device(): lax.all_to_all(cot_rows, ('lat', 'lon'), split_axis=0, concat_axis=0, til...  9.32 us
  transfers between devices with their start and end apart: 6, of which 2 were waited for; matrix products, arithmetic and copies ran while one was open for 38% of the time, Pallas kernels for 0%

profile of v1, /device:TPU:0, one launch (start us, length us, event | category | flops | bytes accessed | tf_op | source)
XLA Modules:
  0.0 318.0 jit_solution(5604382808587441028)
XLA Ops:
  9.9 2.5 collective-permute-start
  14.4 2.3 copy.37
  16.7 9.3 %all-to-all-start = ((bf16[32,64,256]{2,1,0:T(8,128)(2,1)}), bf16[32,64,256]{2,1,0:T(8,128)(2,1)}, u32[]{:S(2)}, u32[]{:S(2)}) async-start(bf16[32,64,256]{2,1,0:T(8,128)(2,1)} %bitcast.110), calls=%async_computation | async-start | bytes 2097152 | tf_op jit(solution)/shard_map/all_to_all | solution.py:72
  30.0 3.6 %fusion.28 = (f32[258,22,3]{2,1,0:T(8,128)}, f32[258,22,3]{2,1,0:T(8,128)}) fusion(f32[258,22,128]{2,1,0:T(8,128)S(1)} %pad_maximum_fusion.1), kind=kLoop, calls=%fused_computation.80 | loop fusion | bytes 272448 | tf_op jit(solution)/shard_map/slice | solution.py:14
  33.6 3.7 %copy.32 = f32[258,22,3]{0,1,2:T(8,128)S(1)} copy(f32[258,22,3]{2,1,0:T(8,128)} %get-tuple-element.32) | data formatting | bytes 136224 | tf_op jit(solution)/shard_map/slice | solution.py:14
  39.1 3.8 %copy.33 = f32[258,22,3]{0,1,2:T(8,128)S(1)} copy(f32[258,22,3]{2,1,0:T(8,128)} %get-tuple-element.33) | data formatting | bytes 136224 | tf_op jit(solution)/shard_map/slice | solution.py:15
  42.9 2.4 collective-permute-start.3
  45.3 5.0 %collective-permute-done.2 = f32[258,22,3]{0,1,2:T(8,128)S(1)} collective-permute-done((f32[258,22,3]{0,1,2:T(8,128)S(1)}, f32[258,22,3]{0,1,2:T(8,128)S(1)}, u32[]{:S(2)}, u32[]{:S(2)}) %collective-permute-start.2) | collective-permute-done | bytes 68144 | tf_op jit(solution)/shard_map/ppermute | solution.py:16
  50.3 3.5 %copy.34 = f32[258,22,3]{2,1,0:T(8,128)} copy(f32[258,22,3]{0,1,2:T(8,128)S(1)} %collective-permute-done.2) | data formatting | bytes 136224 | tf_op jit(solution)/shard_map/ppermute | solution.py:16
  53.9 4.3 %copy.35 = f32[258,22,3]{2,1,0:T(8,128)} copy(f32[258,22,3]{0,1,2:T(8,128)} %collective-permute-done.3) | data formatting | bytes 136224 | tf_op jit(solution)/shard_map/ppermute | solution.py:17
  58.2 10.7 %pad_maximum_fusion = f32[258,22,134]{2,1,0:T(8,128)S(1)} fusion(f32[258,22,3]{2,1,0:T(8,128)} %copy.35, f32[258,3,128]{2,1,0:T(4,128)} %copy-done.5, f32[1,16,128]{2,1,0:T(8,128)S(1)} %bitcast.114, f32[1,16,128]{2,1,0:T(8,128)S(1)} %copy-done.13, f32[256,16,128]{2,1,0:T(8,128)S(1)} %copy-done.2, f32[258,3,128]{2,1,0:T(4,128)S(1)} %copy.30, ...), kind=kLoop, calls=%fused_computation.3 | loop fusion | flops 4563504 | bytes 6084672 | tf_op jit(solution)/shard_map/concatenate | solution.py:18
  69.4 3.6 %fusion.7 = f32[256,21,134]{2,1,0:T(8,128)} fusion(f32[258,22,134]{2,1,0:T(8,128)S(1)} %pad_maximum_fusion, f32[21,134]{1,0:T(8,128)S(1)} %maximum_bitcast_fusion.2), kind=kLoop, calls=%fused_computation.23 | loop fusion | flops 1440768 | bytes 8655864 | tf_op jit(solution)/shard_map/mul | solution.py:23
  73.0 4.3 %fusion.6 = f32[256,22,133]{2,1,0:T(8,128)} fusion(f32[258,22,134]{2,1,0:T(8,128)S(1)} %pad_maximum_fusion, f32[22,133]{1,0:T(8,128)S(1)} %bitcast.111), kind=kLoop, calls=%fused_computation.19 | loop fusion | flops 1498112 | bytes 9000376 | tf_op jit(solution)/shard_map/mul | solution.py:24
  77.3 15.5 %slice_subtract_fusion.6 = f32[256,20,132]{2,1,0:T(8,128)S(1)} fusion(f32[256,22,133]{2,1,0:T(8,128)} %fusion.6, f32[256,21,134]{2,1,0:T(8,128)} %fusion.7, f32[258,22,134]{2,1,0:T(8,128)S(1)} %pad_maximum_fusion), kind=kLoop, calls=%fused_computation.16 | loop fusion | flops 2703360 | bytes 16220160 | tf_op jit(solution)/shard_map/sub | solution.py:27
  92.8 3.6 %fusion.5 = f32[256,19,132]{2,1,0:T(8,128)} fusion(f32[256,20,132]{2,1,0:T(8,128)S(1)} %slice_subtract_fusion.6, f32[19,132]{1,0:T(8,128)S(1)} %slice.187), kind=kLoop, calls=%fused_computation.15 | loop fusion | flops 1284096 | bytes 7714608 | tf_op jit(solution)/shard_map/mul | solution.py:23
  96.4 4.3 %fusion.4 = f32[256,20,131]{2,1,0:T(8,128)} fusion(f32[256,20,132]{2,1,0:T(8,128)S(1)} %slice_subtract_fusion.6, f32[20,131]{1,0:T(8,128)S(1)} %slice.192), kind=kLoop, calls=%fused_computation.11 | loop fusion | flops 1341440 | bytes 8059120 | tf_op jit(solution)/shard_map/mul | solution.py:24
  100.7 15.7 %slice_subtract_fusion.2 = f32[256,18,130]{2,1,0:T(8,128)S(1)} fusion(f32[256,20,131]{2,1,0:T(8,128)} %fusion.4, f32[256,19,132]{2,1,0:T(8,128)} %fusion.5, f32[256,20,132]{2,1,0:T(8,128)S(1)} %slice_subtract_fusion.6), kind=kLoop, calls=%fused_computation.8 | loop fusion | flops 2396160 | bytes 14376960 | tf_op jit(solution)/shard_map/sub | solution.py:27
  116.4 4.0 %fusion.3 = f32[256,17,130]{2,1,0:T(8,128)} fusion(f32[256,18,130]{2,1,0:T(8,128)S(1)} %slice_subtract_fusion.2, f32[17,130]{1,0:T(8,128)S(1)} %slice.198), kind=kLoop, calls=%fused_computation.7 | loop fusion | flops 1131520 | bytes 6797960 | tf_op jit(solution)/shard_map/mul | solution.py:23
  120.9 4.3 %fusion.2 = f32[256,18,129]{2,1,0:T(8,128)} fusion(f32[256,18,130]{2,1,0:T(8,128)S(1)} %slice_subtract_fusion.2, f32[18,129]{1,0:T(8,128)S(1)} %slice.203), kind=kLoop, calls=%fused_computation.5 | loop fusion | flops 1188864 | bytes 7142472 | tf_op jit(solution)/shard_map/mul | solution.py:24
  125.2 12.1 %slice_subtract_fusion.10 = f32[256,16,128]{2,1,0:T(8,128)} fusion(f32[256,18,129]{2,1,0:T(8,128)} %fusion.2, f32[256,17,130]{2,1,0:T(8,128)} %fusion.3, f32[256,18,130]{2,1,0:T(8,128)} %copy-done.1), kind=kLoop, calls=%fused_computation.47 | loop fusion | flops 2097152 | bytes 12582912 | tf_op jit(solution)/shard_map/sub | solution.py:27
  137.3 2.0 copy.36
  139.4 3.0 multiply_convert_fusion
  143.8 4.5 %fusion.15 = (bf16[512,2048]{0,1:T(8,128)(2,1)}, f32[2048,512]{1,0:T(8,128)}) fusion(bf16[512,2048]{0,1:T(8,128)(2,1)S(1)} %get-tuple-element.36, bf16[512,512]{1,0:T(8,128)(2,1)S(1)} %copy-done), kind=kOutput, calls=%fused_computation.36 | convolution fusion | flops 1078984704 | bytes 8912896 | tf_op jit(solution)/shard_map/dot_general | solution.py:42
  148.3 5.9 %fusion.17 = bf16[2048,256]{1,0:T(8,128)(2,1)S(1)} fusion(bf16[2048,256]{1,0:T(8,128)(2,1)} %bitcast.14, s32[2048]{0:T(1024)S(1)} %fusion.23), kind=kOutput, calls=%fused_computation.43 | convolution fusion | flops 2152202240 | bytes 2105344 | tf_op jit(solution)/shard_map/dot_general | solution.py:92
  156.1 2.3 fusion.30
  158.3 2.4 fusion.9
  165.2 3.7 %fusion.20 = f32[256,2048]{0,1:T(8,128)} fusion(f32[256,2048]{0,1:T(8,128)S(1)} %bitcast.108, bf16[512,2048]{0,1:T(8,128)(2,1)} %get-tuple-element.38, bf16[256,512]{1,0:T(8,128)(2,1)S(1)} %copy-done.14), kind=kOutput, calls=%fused_computation.46 | convolution fusion | flops 538443776 | bytes 6553600 | tf_op jit(solution)/shard_map/dot_general | solution.py:45
  168.9 3.2 %copy.38 = f32[256,16,128]{2,1,0:T(8,128)} copy(f32[256,16,128]{0,2,1:T(8,128)} %bitcast.109) | data formatting | bytes 4194304
  172.5 45.0 %psum.31 = f32[512]{0:T(512)S(1)} all-reduce(f32[512]{0:T(512)S(1)} %bitcast.117), channel_id=1, replica_groups=mesh['lat'=8,'lon'=4] {'lat','lon'}, use_global_device_ids=true, to_apply=%region_3.4 | all-reduce | flops 512 | bytes 4096 | tf_op jit(solution)/shard_map/psum | solution.py:100
  218.1 86.8 %all-reduce.3.cloned.1.call-done = (f32[512,256]{1,0:T(8,128)}, f32[512,512]{1,0:T(8,128)}, f32[256,512]{1,0:T(8,128)}) async-done(((f32[512,256]{1,0:T(8,128)}, f32[512,512]{1,0:T(8,128)}, f32[256,512]{1,0:T(8,128)}), (f32[512,256]{1,0:T(8,128)}, f32[512,512]{1,0:T(8,128)}, f32[256,512]{1,0:T(8,128)})) %all-reduce.3.cloned.1.call-update) | async-done | bytes 2097168 | tf_op jit(solution)/shard_map/psum | solution.py:100
  304.9 2.3 broadcast_multiply_fusion
  307.2 1.9 broadcast_multiply_fusion.1
  (84 shorter events, 21.9 us)
Async XLA Ops:
  7.2 136.7 %copy-start = (bf16[512,512]{1,0:T(8,128)(2,1)S(1)}, bf16[512,512]{1,0:T(8,128)(2,1)}, u32[]{:S(2)}) copy-start(bf16[512,512]{1,0:T(8,128)(2,1)} %param.16) | copy-start | bytes 1572868
  8.0 5.1 %copy-start.12 = (f32[1,16,128]{2,1,0:T(8,128)}, f32[1,16,128]{2,1,0:T(8,128)S(1)}, u32[]{:S(2)}) copy-start(f32[1,16,128]{2,1,0:T(8,128)S(1)} %select_bitcast_fusion) | copy-start | bytes 24580
  8.0 18.1 %copy-start.17 = (s32[16,128]{1,0:T(8,128)S(1)}, s32[16,128]{1,0:T(8,128)}, u32[]{:S(2)}) copy-start(s32[16,128]{1,0:T(8,128)} %param.13) | copy-start | bytes 24580
  9.8 19.0 %copy-start.2 = (f32[256,16,128]{2,1,0:T(8,128)S(1)}, f32[256,16,128]{2,1,0:T(8,128)}, u32[]{:S(2)}) copy-start(f32[256,16,128]{2,1,0:T(8,128)} %param.10) | copy-start | bytes 6291460
  9.9 16.8 %collective-permute-start = (f32[258,3,128]{2,0,1:T(8,128)S(1)}, f32[258,3,128]{2,0,1:T(8,128)S(1)}, u32[]{:S(2)}, u32[]{:S(2)}) collective-permute-start(f32[258,3,128]{2,0,1:T(8,128)S(1)} %copy.28), channel_id=1, source_target_pairs={{0,4},{4,8},{8,12},{12,16},{16,20},{20,24},{24,28},{1,5},{5,9},{9,... | collective-permute-start | bytes 1188872 | tf_op jit(solution)/shard_map/ppermute | solution.py:16
  13.2 13.7 %collective-permute-start.1 = (f32[258,3,128]{2,0,1:T(8,128)}, f32[258,3,128]{2,0,1:T(8,128)}, u32[]{:S(2)}, u32[]{:S(2)}) collective-permute-start(f32[258,3,128]{2,0,1:T(8,128)} %copy.29), channel_id=1, source_target_pairs={{4,0},{8,4},{12,8},{16,12},{20,16},{24,20},{28,24},{5,1},{9,5},{13... | collective-permute-start | bytes 1188872 | tf_op jit(solution)/shard_map/ppermute | solution.py:17
  16.7 131.6 %all-to-all-start = ((bf16[32,64,256]{2,1,0:T(8,128)(2,1)}), bf16[32,64,256]{2,1,0:T(8,128)(2,1)}, u32[]{:S(2)}, u32[]{:S(2)}) async-start(bf16[32,64,256]{2,1,0:T(8,128)(2,1)} %bitcast.110), calls=%async_computation | async-start | bytes 2097152 | tf_op jit(solution)/shard_map/all_to_all | solution.py:72
  26.0 278.9 %all-reduce.3.cloned.1.call-start = ((), (), s32[]{:S(2)}) async-start(), calls=%async_computation.1 | async-start | bytes 4194304 | tf_op jit(solution)/shard_map/psum | solution.py:100
  28.0 0.8 copy-start.5
  33.6 11.6 %copy-start.18 = (s32[16,128]{1,0:T(8,128)S(1)}, s32[16,128]{1,0:T(8,128)}, u32[]{:S(2)}) copy-start(s32[16,128]{1,0:T(8,128)} %param.14) | copy-start | bytes 24580
  37.4 12.9 %collective-permute-start.2 = (f32[258,22,3]{0,1,2:T(8,128)S(1)}, f32[258,22,3]{0,1,2:T(8,128)S(1)}, u32[]{:S(2)}, u32[]{:S(2)}) collective-permute-start(f32[258,22,3]{0,1,2:T(8,128)S(1)} %copy.32), channel_id=1, source_target_pairs={{0,1},{1,2},{2,3},{3,0},{4,5},{5,6},{6,7},{7,4},{8,9},{9,10},{10,1... | collective-permute-start | bytes 204344 | tf_op jit(solution)/shard_map/ppermute | solution.py:16
  39.1 19.1 %copy-start.13 = (f32[1,16,128]{2,1,0:T(8,128)S(1)}, f32[1,16,128]{2,1,0:T(8,128)}, u32[]{:S(2)}) copy-start(f32[1,16,128]{2,1,0:T(8,128)} %copy-done.12) | copy-start | bytes 24580
  39.1 19.1 %copy-start.15 = (f32[16,128]{1,0:T(8,128)S(1)}, f32[16,128]{1,0:T(8,128)}, u32[]{:S(2)}) copy-start(f32[16,128]{1,0:T(8,128)} %param.12) | copy-start | bytes 24580
  42.9 11.0 %collective-permute-start.3 = (f32[258,22,3]{0,1,2:T(8,128)S(1)}, f32[258,22,3]{0,1,2:T(8,128)}, u32[]{:S(2)}, u32[]{:S(2)}) collective-permute-start(f32[258,22,3]{0,1,2:T(8,128)S(1)} %copy.33), channel_id=1, source_target_pairs={{1,0},{2,1},{3,2},{0,3},{5,4},{6,5},{7,6},{4,7},{9,8},{10,9},{11,1... | collective-permute-start | bytes 204344 | tf_op jit(solution)/shard_map/ppermute | solution.py:17
  58.2 10.7 %copy-start.3 = (f32[258,22,3]{2,1,0:T(8,128)S(1)}, f32[258,22,3]{2,1,0:T(8,128)}, u32[]{:S(2)}) copy-start(f32[258,22,3]{2,1,0:T(8,128)} %copy.34) | copy-start | bytes 204340
  58.2 10.7 %copy-start.4 = (f32[258,22,3]{2,1,0:T(8,128)S(1)}, f32[258,22,3]{2,1,0:T(8,128)}, u32[]{:S(2)}) copy-start(f32[258,22,3]{2,1,0:T(8,128)} %copy.35) | copy-start | bytes 204340
  58.2 10.7 %copy-start.6 = (f32[258,3,128]{2,1,0:T(4,128)S(1)}, f32[258,3,128]{2,1,0:T(4,128)}, u32[]{:S(2)}) copy-start(f32[258,3,128]{2,1,0:T(4,128)} %copy-done.5) | copy-start | bytes 1188868
  116.4 4.5 %copy-start.1 = (f32[256,18,130]{2,1,0:T(8,128)}, f32[256,18,130]{2,1,0:T(8,128)S(1)}, u32[]{:S(2)}) copy-start(f32[256,18,130]{2,1,0:T(8,128)S(1)} %slice_subtract_fusion.2) | copy-start | bytes 7188484
  137.3 2.1 copy-start.19
  137.3 2.1 copy-start.20
  137.3 2.1 copy-start.21
  139.4 3.0 copy-start.9
  142.4 1.4 copy-start.22
  148.3 5.9 %copy-start.14 = (bf16[256,512]{1,0:T(8,128)(2,1)S(1)}, bf16[256,512]{1,0:T(8,128)(2,1)}, u32[]{:S(2)}) copy-start(bf16[256,512]{1,0:T(8,128)(2,1)} %param.17) | copy-start | bytes 786436
  148.3 5.9 %copy-start.25 = (f32[2048,512]{1,0:T(8,128)S(1)}, f32[2048,512]{1,0:T(8,128)}, u32[]{:S(2)}) copy-start(f32[2048,512]{1,0:T(8,128)} %get-tuple-element.39) | copy-start | bytes 12582916
  154.3 1.8 copy-start.23
  156.1 2.3 copy-start.24
  158.3 3.8 %copy-start.10 = (bf16[256,2048]{0,1:T(8,128)(2,1)S(1)}, bf16[256,2048]{0,1:T(8,128)(2,1)}, u32[]{:S(2)}) copy-start(bf16[256,2048]{0,1:T(8,128)(2,1)} %copy-done.9) | copy-start | bytes 3145732
  158.3 5.3 %copy-start.11 = (bf16[512,2048]{0,1:T(8,128)(2,1)S(1)}, bf16[512,2048]{0,1:T(8,128)(2,1)}, u32[]{:S(2)}) copy-start(bf16[512,2048]{0,1:T(8,128)(2,1)} %get-tuple-element.38) | copy-start | bytes 6291460
  160.8 1.4 copy-start.7
  162.1 3.1 copy-start.16
  168.9 3.2 %copy-start.8 = (bf16[512,2048]{0,1:T(8,128)(2,1)S(1)}, bf16[512,2048]{0,1:T(8,128)(2,1)}, u32[]{:S(2)}) copy-start(bf16[512,2048]{0,1:T(8,128)(2,1)} %copy-done.7) | copy-start | bytes 6291460
Sparse Core Ops, SparseCore 0:
  165.3 139.5 all-reduce.2

commit v2 on v1

v2 whole, which is shorter than its diff:
```python
import functools

import jax
import jax.numpy as jnp
from jax import lax
from jax.experimental import pallas as pl
from jax.experimental.pallas import tpu as pltpu
from jax.sharding import PartitionSpec as P

SUBSTEPS = 3
PAD = 16
F32 = jnp.float32
BF16 = jnp.bfloat16


def iota(shape, dim):
    return lax.broadcasted_iota(jnp.int32, shape, dim)


def dot(a, b):
    return jnp.dot(a, b, preferred_element_type=F32)


def dot_nt(a, b):
    return lax.dot_general(a, b, (((1,), (1,)), ((), ())), preferred_element_type=F32)


def kernel(
    n_lat,
    n_lon,
    state,
    north,
    east,
    land,
    place,
    w_in,
    w_mid,
    w_out,
    w_land,
    cot,
    new_state,
    grads,
    grad_land,
    ext,
    cn_ext,
    ce_ext,
    edge_rows,
    packed,
    halo_rx,
    pack_rx,
    strip_w,
    strip_e,
    cot_tx,
    cot_rx,
    cot_pl,
    pick,
    feeds,
    act1,
    act2,
    der1,
    der2,
    wt_out,
    wt_mid,
    part,
    land_acc,
    sum0,
    sum1,
    rx0,
    rx1,
    rx2,
    tx0,
    tx1,
    tx2,
    state_sem,
    out_sem,
    halo_send,
    halo_recv,
    a2a_send,
    a2a_recv,
    red_send,
    red_recv,
    gat_send,
    gat_recv,
):
    channels, rows, cols = state.shape
    devs = n_lat * n_lon
    columns = rows * cols
    block = columns // devs
    lat, lon = lax.axis_index("lat"), lax.axis_index("lon")
    me = lat * n_lon + lon

    def place_of(d):
        return (d // n_lon, lax.rem(d, n_lon))

    loads = [
        pltpu.make_async_copy(state.at[:, r, :], ext.at[r + 3], state_sem.at[r])
        for r in range(rows)
    ]
    for copy in loads:
        copy.start()

    barrier = pltpu.get_barrier_semaphore()

    @pl.loop(1, devs)
    def _(k):
        pl.semaphore_signal(
            barrier,
            inc=1,
            device_id=place_of(lax.rem(me + k, devs)),
            device_id_type=pl.DeviceIdType.MESH,
        )

    n_all, e_all = north[...], east[...]
    n_hi, e_hi = n_all.astype(BF16).astype(F32), e_all.astype(BF16).astype(F32)
    n_lo, e_lo = n_all - n_hi, e_all - e_hi
    sub = iota((PAD, cols), 0)
    kk, ll = iota((cols, cols), 0), iota((cols, cols), 1)
    spot = jnp.where(kk < 3, kk, jnp.where(kk >= cols - 3, kk - (cols - 6), -1000))
    cn_ext[3 : 3 + rows] = n_all
    ce_ext[3 : 3 + rows] = e_all
    total = jnp.zeros((channels + PAD, cols), F32)
    for r in range(rows):
        loads[r].wait()
        coef = jnp.where(
            sub == 0,
            n_hi[r : r + 1],
            jnp.where(
                sub == 1,
                n_lo[r : r + 1],
                jnp.where(sub == 2, e_hi[r : r + 1], jnp.where(sub == 3, e_lo[r : r + 1], 0.0)),
            ),
        )
        tile = jnp.concatenate([ext[r + 3].astype(BF16), coef.astype(BF16)], 0)
        if r < 3:
            edge_rows[0, r] = tile
        if r >= rows - 3:
            edge_rows[1, r - (rows - 3)] = tile
        total += dot(tile, (ll == spot + 6 * r).astype(BF16))
    packed[...] = total.astype(BF16)

    pl.semaphore_wait(barrier, devs - 1)
    up, down = lax.rem(lat + 1, n_lat), lax.rem(lat + n_lat - 1, n_lat)
    right, left = lax.rem(lon + 1, n_lon), lax.rem(lon + n_lon - 1, n_lon)
    sends = [
        (edge_rows.at[1], halo_rx.at[0], (up, lon)),
        (edge_rows.at[0], halo_rx.at[1], (down, lon)),
        (packed, pack_rx.at[0], (lat, right)),
        (packed, pack_rx.at[1], (lat, left)),
        (packed, pack_rx.at[2], (up, right)),
        (packed, pack_rx.at[3], (down, right)),
        (packed, pack_rx.at[4], (up, left)),
        (packed, pack_rx.at[5], (down, left)),
    ]
    halos = [
        pltpu.make_async_remote_copy(
            src_ref=src,
            dst_ref=dst,
            send_sem=halo_send.at[i],
            recv_sem=halo_recv.at[i],
            device_id=where,
            device_id_type=pl.DeviceIdType.MESH,
        )
        for i, (src, dst, where) in enumerate(sends)
    ]
    for copy in halos:
        copy.start()

    for j in range(columns // 128):
        cot_tx[j * 128 : (j + 1) * 128] = cot[:, j * 128 : (j + 1) * 128].T

    def exchange(k):
        there = lax.rem(me + k, devs)
        return pltpu.make_async_remote_copy(
            src_ref=cot_tx.at[pl.ds(pl.multiple_of(there * block, block), block)],
            dst_ref=cot_rx.at[pl.ds(pl.multiple_of(me * block, block), block)],
            send_sem=a2a_send.at[k],
            recv_sem=a2a_recv.at[me],
            device_id=place_of(there),
            device_id_type=pl.DeviceIdType.MESH,
        )

    def arrival(k):
        source = lax.rem(me + k, devs)
        return pltpu.make_async_remote_copy(
            src_ref=cot_tx.at[pl.ds(0, block)],
            dst_ref=cot_rx.at[pl.ds(pl.multiple_of(source * block, block), block)],
            send_sem=a2a_send.at[k],
            recv_sem=a2a_recv.at[source],
            device_id=place_of(source),
            device_id_type=pl.DeviceIdType.MESH,
        )

    @pl.loop(1, devs)
    def _(k):
        exchange(k).start()

    own = pl.ds(pl.multiple_of(me * block, block), block)
    cot_rx[own] = cot_tx[own]
    wt_out[...] = w_out[...].T
    wt_mid[...] = w_mid[...].T

    for copy in halos:
        copy.wait()
    for side, first in ((0, 0), (1, rows + 3)):
        for j in range(3):
            tile = halo_rx[side, j].astype(F32)
            ext[first + j] = tile[:channels]
            cn_ext[first + j : first + j + 1] = tile[channels : channels + 1] + tile[channels + 1 : channels + 2]
            ce_ext[first + j : first + j + 1] = tile[channels + 2 : channels + 3] + tile[channels + 3 : channels + 4]

    rest = kk - 6 * ((kk * 43) >> 8)
    low = (rest < 3) & (kk < 6 * rows)
    high = (rest >= 3) & (kk < 6 * rows)
    top, bottom = kk >= 6 * (rows - 2), kk < 12
    far = 6 * (rows + 2)

    def chosen(mask, offset):
        return (mask & (ll == kk + offset)).astype(BF16)

    last = 6 * (rows - 2)
    outer = [(halo_rx[0, 1], 0), (halo_rx[0, 2], 6), (halo_rx[1, 0], far), (halo_rx[1, 1], far + 6)]
    west = dot(packed[...], chosen(low, 15)) + dot(pack_rx[0], chosen(high, 9))
    west += dot(pack_rx[2], chosen(high & top, -last - 3)) + dot(pack_rx[3], chosen(high & bottom, far - 3))
    for tile, base in outer:
        west += dot(tile, chosen(kk < 3, base + 3))
    strip_w[...] = west
    right_side = dot(packed[...], chosen(high, 9)) + dot(pack_rx[1], chosen(low, 15))
    right_side += dot(pack_rx[4], chosen(low & top, 3 - last)) + dot(pack_rx[5], chosen(low & bottom, far + 3))
    for tile, base in outer:
        right_side += dot(tile, chosen(kk >= cols - 3, base - (cols - 3)))
    strip_e[...] = right_side

    chunk = 64
    lane = iota((chunk, cols), 1)

    def turn(x, by):
        return pltpu.roll(x, by % cols, 1)

    @pl.loop(0, channels // chunk)
    def _(c):
        here = pl.ds(pl.multiple_of(c * chunk, chunk), chunk)
        strips = []
        for ref in (strip_w, strip_e):
            cn = ref[channels : channels + 1] + ref[channels + 1 : channels + 2]
            ce = ref[channels + 2 : channels + 3] + ref[channels + 3 : channels + 4]
            strips.append([ref[here], cn, ce])
        for step in range(SUBSTEPS):
            fluxes = []
            for strip in strips:
                f, cn, ce = strip
                fluxes.append(ce * (turn(f, -1) - f))
            west_flux, east_value = fluxes[0], strips[1][0]
            if step < SUBSTEPS - 1:
                for strip, fe in zip(strips, fluxes):
                    f, cn, ce = strip
                    fn = cn * (turn(f, -6) - f)
                    strip[0] = f + fn - turn(fn, 6) + fe - turn(fe, 1)
            f = ext[step, here]
            nxt = ext[step + 1, here]
            fn_before = cn_ext[step : step + 1] * (nxt - f)
            for e in range(step + 1, rows + 5 - step):
                f = nxt
                nxt = ext[e + 1, here]
                at = 6 * (e - 1)
                fn = cn_ext[e : e + 1] * (nxt - f)
                f_east = jnp.where(lane == cols - 1, turn(east_value, cols - 1 - (at + 3)), turn(f, -1))
                fe = ce_ext[e : e + 1] * (f_east - f)
                fe_before = jnp.where(lane == 0, turn(west_flux, -(at + 2)), turn(fe, 1))
                ext[e, here] = f + fn - fn_before + fe - fe_before
                fn_before = fn

    wide = 256
    per = wide // cols
    for t in range(columns // wide):
        for j in range(per):
            r = t * per + j
            feeds[:, r * cols : (r + 1) * cols] = ext[r + 3].astype(BF16)

    tiles = columns // wide
    kind = iota((columns, wide), 0)

    @pl.loop(0, tiles)
    def _(t):
        at = pl.ds(pl.multiple_of(t * wide, wide), wide)
        pre = dot(w_in[...], feeds[:, at]) + w_land[...] * land[:, at]
        sig = 0.5 * jnp.tanh(0.5 * pre) + 0.5
        act = pre * sig
        a1 = act.astype(BF16)
        act1[:, at] = a1
        der1[:, at] = sig * (1.0 + pre - act)
        pre = dot(w_mid[...], a1)
        sig = 0.5 * jnp.tanh(0.5 * pre) + 0.5
        act = pre * sig
        a2 = act.astype(BF16)
        act2[:, at] = a2
        der2[:, at] = sig * (1.0 + pre - act)
        tend = dot(w_out[...], a2).astype(BF16).astype(F32)
        for j in range(per):
            ext[t * per + j + 3] += tend[:, j * cols : (j + 1) * cols]
        pick[:, at] = jnp.where(kind == place[:, at], 1.0, 0.0).astype(BF16)

    stores = [
        pltpu.make_async_copy(ext.at[r + 3], new_state.at[:, r, :], out_sem.at[r])
        for r in range(rows)
    ]
    for copy in stores:
        copy.start()

    part[...] = jnp.zeros_like(part)
    land_acc[...] = jnp.zeros_like(land_acc)

    @pl.loop(1, devs)
    def _(k):
        arrival(k).wait_recv()

    for j in range(columns // 128):
        cot_pl[:, j * 128 : (j + 1) * 128] = cot_rx[j * 128 : (j + 1) * 128].T

    hidden = w_in.shape[0]
    half = hidden // 2

    @pl.loop(0, tiles)
    def _(t):
        at = pl.ds(pl.multiple_of(t * wide, wide), wide)
        cg = dot(cot_pl[...], pick[:, at]).astype(BF16)
        out = dot_nt(cg, act2[:, at])
        part[4 * hidden - 2 * half : 4 * hidden - half] += out[:, :half]
        part[4 * hidden - half : 4 * hidden] += out[:, half:]
        b2 = (dot(wt_out[...], cg) * der2[:, at]).astype(BF16)
        mid = dot_nt(b2, act1[:, at])
        part[hidden : 2 * hidden] += mid[:, :half]
        part[2 * hidden : 3 * hidden] += mid[:, half:]
        b1f = dot(wt_mid[...], b2) * der1[:, at]
        b1 = b1f.astype(BF16)
        part[:hidden] += dot_nt(b1, feeds[:, at])
        weighed = b1.astype(F32) * land[:, at]
        gathered = weighed[:, :128]
        for j in range(1, wide // 128):
            gathered += weighed[:, j * 128 : (j + 1) * 128]
        land_acc[...] += gathered

    vec = jnp.sum(land_acc[...].T, axis=0, keepdims=True)
    sub_w = iota((PAD, half), 0)
    land_rows = jnp.where(sub_w == 0, vec[:, :half], jnp.where(sub_w == 1, vec[:, half:], 0.0))

    pairs = n_lat // 2
    core, chip = lax.rem(lat, 2), lat // 2
    levels = [
        (2, core, lambda p: (chip * 2 + p, lon), tx0, rx0, part, sum0, 0),
        (pairs, chip, lambda p: (p * 2 + core, lon), tx1, rx1, sum0, sum1, 1),
        (n_lon, lon, lambda p: (lat, p), tx2, rx2, sum1, None, 1 + pairs - 1),
    ]
    for size, mine, where, tx, rx, src, dst, base in levels:
        share = tx.shape[1] - PAD
        extra = land_rows.astype(BF16)
        for p in range(size):
            tx[p, :share] = src[p * share : (p + 1) * share].astype(BF16)
            tx[p, share:] = extra
        copies = []
        for k in range(1, size):
            there = lax.rem(mine + k, size)
            copies.append(
                pltpu.make_async_remote_copy(
                    src_ref=tx.at[there],
                    dst_ref=rx.at[size - 1 - k],
                    send_sem=red_send.at[base + k - 1],
                    recv_sem=red_recv.at[base + size - 1 - k],
                    device_id=where(there),
                    device_id_type=pl.DeviceIdType.MESH,
                )
            )
        for copy in copies:
            copy.start()
        for copy in copies:
            copy.wait()
        summed = tx[mine, :share].astype(F32)
        for s in range(size - 1):
            summed += rx[s, :share].astype(F32)
        land_rows = jnp.zeros((PAD, half), F32)
        for p in range(size):
            slot = lax.rem(p - mine - 1 + 2 * size, size)
            theirs = rx[jnp.minimum(slot, size - 2), share:].astype(F32)
            land_rows += jnp.where(p == mine, extra.astype(F32), theirs)
        if dst is not None:
            dst[...] = summed

    shares = [tx0.shape[1] - PAD, tx1.shape[1] - PAD, tx2.shape[1] - PAD]
    start0 = core * shares[0]
    start1 = start0 + chip * shares[1]
    start2 = start1 + lon * shares[2]
    grads[pl.ds(pl.multiple_of(start2, shares[2]), shares[2])] = summed.astype(BF16)
    grad_land[...] = land_rows
    spread = [
        (n_lon, lon, lambda p: (lat, p), start1, start2, shares[2], 0),
        (pairs, chip, lambda p: (p * 2 + core, lon), start0, start1, shares[1], n_lon - 1),
        (2, core, lambda p: (chip * 2 + p, lon), 0, start0, shares[0], n_lon + pairs - 2),
    ]
    for size, mine, where, group, start, share, base in spread:
        copies, waits = [], []
        for k in range(1, size):
            there = lax.rem(mine + k, size)
            piece = grads.at[pl.ds(pl.multiple_of(start, share), share)]
            landing = grads.at[pl.ds(pl.multiple_of(group + there * share, share), share)]
            copies.append(
                pltpu.make_async_remote_copy(
                    src_ref=piece,
                    dst_ref=piece,
                    send_sem=gat_send.at[base + k - 1],
                    recv_sem=gat_recv.at[base + size - 1 - k],
                    device_id=where(there),
                    device_id_type=pl.DeviceIdType.MESH,
                )
            )
            waits.append(
                pltpu.make_async_remote_copy(
                    src_ref=piece,
                    dst_ref=landing,
                    send_sem=gat_send.at[base + k - 1],
                    recv_sem=gat_recv.at[base + k - 1],
                    device_id=where(there),
                    device_id_type=pl.DeviceIdType.MESH,
                )
            )
        for copy in copies:
            copy.start()
        for copy in waits:
            copy.wait_recv()
        for copy in copies:
            copy.wait_send()

    @pl.loop(1, devs)
    def _(k):
        exchange(k).wait_send()

    for copy in stores:
        copy.wait()


def per_device(
    n_lat,
    n_lon,
    state,
    north_coef,
    east_coef,
    land_mask,
    owner_slot,
    w_in,
    w_mid,
    w_out,
    w_land,
    tend_cot,
):
    channels, rows, cols = state.shape
    hidden = w_in.shape[0]
    devs = n_lat * n_lon
    columns = rows * cols
    block = columns // devs
    row_index = lax.axis_index("lat") * rows + jnp.arange(rows, dtype=jnp.int32)
    north_face = jnp.where(row_index[:, None] < rows * n_lat - 1, north_coef, jnp.float32(0.0))
    slots = owner_slot.reshape(1, columns)
    place = slots // columns * block + slots % block
    land = land_mask.reshape(1, columns).astype(F32)
    total = 4 * hidden
    half = hidden // 2
    share0, share1, share2 = total // 2, total // n_lat, total // devs
    pairs = n_lat // 2
    tall = channels + PAD
    vmem = pl.BlockSpec(memory_space=pltpu.VMEM)
    anyspace = pl.BlockSpec(memory_space=pl.ANY)
    red = 1 + (pairs - 1) + (n_lon - 1)
    dma = pltpu.SemaphoreType.DMA
    new_state, grads, grad_land = pl.pallas_call(
        functools.partial(kernel, n_lat, n_lon),
        out_shape=(
            jax.ShapeDtypeStruct(state.shape, F32),
            jax.ShapeDtypeStruct((total, half), BF16),
            jax.ShapeDtypeStruct((PAD, half), F32),
        ),
        in_specs=[anyspace] + [vmem] * 9,
        out_specs=(anyspace, vmem, vmem),
        scratch_shapes=[
            pltpu.VMEM((rows + 6, channels, cols), F32),
            pltpu.VMEM((rows + 8, cols), F32),
            pltpu.VMEM((rows + 8, cols), F32),
            pltpu.VMEM((2, 3, tall, cols), BF16),
            pltpu.VMEM((tall, cols), BF16),
            pltpu.VMEM((2, 3, tall, cols), BF16),
            pltpu.VMEM((6, tall, cols), BF16),
            pltpu.VMEM((tall, cols), F32),
            pltpu.VMEM((tall, cols), F32),
            pltpu.VMEM((columns, channels), BF16),
            pltpu.VMEM((columns, channels), BF16),
            pltpu.VMEM((channels, columns), BF16),
            pltpu.VMEM((columns, columns), BF16),
            pltpu.VMEM((channels, columns), BF16),
            pltpu.VMEM((hidden, columns), BF16),
            pltpu.VMEM((hidden, columns), BF16),
            pltpu.VMEM((hidden, columns), F32),
            pltpu.VMEM((hidden, columns), F32),
            pltpu.VMEM((hidden, channels), BF16),
            pltpu.VMEM((hidden, hidden), BF16),
            pltpu.VMEM((total, half), F32),
            pltpu.VMEM((hidden, 128), F32),
            pltpu.VMEM((share0, half), F32),
            pltpu.VMEM((share1, half), F32),
            pltpu.VMEM((1, share0 + PAD, half), BF16),
            pltpu.VMEM((pairs - 1, share1 + PAD, half), BF16),
            pltpu.VMEM((n_lon - 1, share2 + PAD, half), BF16),
            pltpu.VMEM((2, share0 + PAD, half), BF16),
            pltpu.VMEM((pairs, share1 + PAD, half), BF16),
            pltpu.VMEM((n_lon, share2 + PAD, half), BF16),
            dma((rows,)),
            dma((rows,)),
            dma((8,)),
            dma((8,)),
            dma((devs,)),
            dma((devs,)),
            dma((red,)),
            dma((red,)),
            dma((red,)),
            dma((red,)),
        ],
        compiler_params=pltpu.CompilerParams(
            collective_id=0, has_side_effects=True, vmem_limit_bytes=56 * 1024 * 1024
        ),
    )(
        state,
        north_face,
        east_coef,
        land,
        place,
        w_in,
        w_mid,
        w_out,
        w_land.reshape(hidden, 1),
        tend_cot,
    )
    scale = jnp.float32((columns * devs) ** (-0.5))
    wide = grads.astype(F32) * scale
    grad_in = wide[:hidden]
    grad_mid = jnp.concatenate([wide[hidden : 2 * hidden], wide[2 * hidden : 3 * hidden]], 1)
    grad_out = jnp.concatenate([wide[3 * hidden : 3 * hidden + half], wide[3 * hidden + half :]], 1)
    return new_state, grad_in, grad_mid, grad_out, grad_land[:2].reshape(hidden) * scale


def solution(mesh):
    n_lat, n_lon = mesh.shape["lat"], mesh.shape["lon"]
    placed = (
        P(None, "lat", "lon"),
        P("lat", "lon"),
        P("lat", "lon"),
        P("lat", "lon"),
        P("lat", "lon"),
        P(),
        P(),
        P(),
        P(),
        P(None, ("lat", "lon")),
    )
    return jax.shard_map(
        functools.partial(per_device, n_lat, n_lon),
        mesh=mesh,
        in_specs=placed,
        out_specs=(P(None, "lat", "lon"), P(), P(), P(), P()),
        check_vma=False,
    )
```

time: 323 us -> 108 us (0.33); the launches traced: 318 us -> 107 us
  Pallas kernels: 0 us -> 94.2 us
  waiting for transfers between devices: 91.9 us -> 0 us
  other arithmetic: 89.3 us -> 8.06 us
  blocking collectives: 45 us -> 0 us
  local copies, waits for them, and re-layouts: 32.9 us -> 4.37 us
  matrix products: 27 us -> 0 us
  starting transfers between devices: 17.3 us -> 0 us
  between operations: 14.6 us -> 0.67 us
    pallas_call x0 -> x1, Pallas kernels: none -> 94.2 us  [per_device(): pl.pallas_call(functools.partial(kernel, n_lat, n_lon), out_shape=(jax.Sh...]
    psum x1 -> x0, waiting for transfers between devices: 86.8 us -> none  [per_device(): summed = lax.psum(gradients, ('lat', 'lon'))]
    psum x1 -> x0, blocking collectives: 45 us -> none  [per_device(): summed = lax.psum(gradients, ('lat', 'lon'))]
    sub x3 -> x0, other arithmetic: 43.2 us -> none  [advance(): inner + flux_north[:, 1:, 1:-1] - flux_north[:, :-1, 1:-1]]
    mul x11 -> x1, other arithmetic: 30.9 us -> 1.36 us  [per_device(): wide = grads.astype(F32) * scale]
    dot_general x10 -> x0, matrix products: 27 us -> none  [the longest x1 5.9 us: per_device(): lax.dot_general(cot_rows, pick, (((0,), (0,)), ((), ())), preferred_eleme...]
    slice x9 -> x2, local copies, waits for them, and re-layouts: 12.2 us -> 0.93 us  [the longest x1 0.9 us: per_device(): wide[hidden:2 * hidden]]
    concatenate x2, other arithmetic: 11.9 us -> 1.98 us  [the longest x1 1.12 us: per_device(): jnp.concatenate([wide[hidden:2 * hidden], wide[2 * hidden:3 * hidden]], 1)]
  transfers between devices with their start and end apart: 6 -> 0, of which waited for: 2 -> 0; matrix products, arithmetic and copies ran while one was open for 38% -> 0% of each run, Pallas kernels for 0% -> 0%
where the time goes in v2:
time: 108 us; the launch traced here: 107 us
  Pallas kernels  94.2 us (87%)
  other arithmetic  8.06 us (7%)
  local copies, waits for them, and re-layouts  4.37 us (4%)
    pallas_call x1, Pallas kernels, per_device(): pl.pallas_call(functools.partial(kernel, n_lat, n_lon), out_shape=(jax.Sh...  94.2 us

profile of v2, /device:TPU:0, one launch (start us, length us, event | category | flops | bytes accessed | tf_op | source)
XLA Modules:
  0.0 107.3 jit_solution(11414369586487342183)
XLA Ops:
  0.6 1.4 %broadcast_select_fusion.north = f32[16,128]{1,0:T(8,128)} fusion(f32[16,128]{1,0:T(8,128)} %param.11, pred[16]{0:T(512)(128)(4,1)S(1)} %add_compare_fusion), kind=kLoop, calls=%fused_computation.10 | loop fusion | flops 2048 | bytes 16400 | tf_op jit(solution)/shard_map/jit(_where)/select_n | solution.py:459
  2.0 1.3 %convert_element_type.8 = f32[16,128]{1,0:T(8,128)} convert(s32[16,128]{1,0:T(8,128)} %param.13) | non-fusion elementwise | flops 2048 | bytes 16384 | tf_op jit(solution)/shard_map/convert_element_type | solution.py:462
  3.3 1.4 %fusion.place = s32[1,2048]{1,0:T(1,128)} fusion(s32[1,2048]{1,0:T(1,128)} %bitcast.7), kind=kLoop, calls=%fused_computation.9 | loop fusion | flops 51200 | bytes 16384 | tf_op jit(solution)/shard_map/add | solution.py:461
  4.7 1.5 %copy.15.w_land = f32[512,1]{1,0:T(8,128)} copy(f32[512,1]{0,1:T(1,128)} %bitcast.8) | data formatting | bytes 4096 | tf_op jit(solution)/shard_map/reshape | solution.py:535
  6.2 94.2 %shard_map.137 = (f32[256,16,128]{2,1,0:T(8,128)}, bf16[2048,256]{1,0:T(8,128)(2,1)}, f32[16,256]{1,0:T(8,128)}) custom-call(f32[256,16,128]{2,1,0:T(8,128)} %state.1, f32[16,128]{1,0:T(8,128)} %broadcast_select_fusion.north, f32[16,128]{1,0:T(8,128)} %east.1, f32[1,2048]{1,0:T(1,128)} %bitcast.6, s32[1,2048]{1,0:T(1,128)} %fusion.place, ...), custom_call_target="tpu_custom_call" | custom-call | tf_op jit(solution)/shard_map/pallas_call | solution.py:472
  100.4 0.7 multiply_bitcast_fusion
  101.1 0.6 copy.16
  101.7 1.4 %convert_multiply_fusion = f32[2048,256]{1,0:T(8,128)S(1)} fusion(bf16[2048,256]{1,0:T(8,128)(2,1)} %get-tuple-element.9), kind=kLoop, calls=%fused_computation | loop fusion | flops 1048576 | bytes 3145728 | tf_op jit(solution)/shard_map/mul | solution.py:539
  103.1 0.9 fusion.2
  104.0 0.0 copy-start
  104.0 1.1 %pad_maximum_fusion = f32[512,512]{1,0:T(8,128)} fusion(f32[512,256]{1,0:T(8,128)S(1)} %get-tuple-element.14, f32[512,256]{1,0:T(8,128)S(1)} %get-tuple-element.13), kind=kLoop, calls=%fused_computation.1 | loop fusion | flops 262144 | bytes 2097152 | tf_op jit(solution)/shard_map/concatenate | solution.py:541
  105.2 0.9 pad_maximum_fusion.1
  106.0 0.0 copy-done
  106.0 1.3 %copy.18 = f32[256,16,128]{2,1,0:T(8,128)} copy(f32[256,16,128]{2,1,0:T(8,128)S(1)} %copy-done) | data formatting | bytes 4194304
  (2 shorter events, 0.0 us)
Async XLA Ops:
  104.0 2.0 %copy-start = (f32[256,16,128]{2,1,0:T(8,128)S(1)}, f32[256,16,128]{2,1,0:T(8,128)}, u32[]{:S(2)}) copy-start(f32[256,16,128]{2,1,0:T(8,128)} %get-tuple-element.21) | copy-start | bytes 6291460
